TPU v7x, 512 devices: a whole 4x8x8 slice. The times are simulated.
512 devices in a mesh: row: 32 (over x, z_lo, core), col: 16 (over y, z_hi).
Axes of the slice: x: 4, y: 8, z: 8 (z_hi: 2, z_lo: 4; z = z_hi * 4 + z_lo), core: 2. Of those that a mesh axis runs over, the one named last changes fastest.
Arguments:
- omega: bfloat16 [32768, 256], P('row'), may hold values from -6 to 6
- psi: bfloat16 [32768, 256], P('col'), may hold values from -6 to 6
- near_tiles: bfloat16 [32768, 1536], P('row'), may hold values from -0.15625 to 0.15625
- left_factors: bfloat16 [32768, 4096], P('row', 'col'), may hold values from -0.09375 to 0.09375
- right_factors: bfloat16 [4096, 32768], P('row', 'col'), may hold values from -0.25 to 0.25
- admissible: int32 [64, 64], P('row', 'col'), may hold values from 0 to 1, as said below
- ranks: int32 [64, 64], P('row', 'col'), may hold values from 8 to 64, as said below
Outputs:
- samples_right: float32 [32768, 256], P(('row', 'col'))
- samples_left: float32 [32768, 256], P(('col', 'row'))
Inputs may be any that keep to these rules, and one draw needn't show every extreme that they name: `admissible`: 0 only where the tiles' indices differ by at most 1; every diagonal tile is 0. `ranks`: some tile has rank 64.
All inputs are finite; a program needn't handle non-finite values.
Results may differ from a plain program's by a relative error of at most 0.0018.
Values may be sent and summed in bfloat16 or wider, within the bound.
A program may use at most 64 MiB of HBM per device.

v0:
```python
import jax
import jax.numpy as jnp
from jax import lax
from jax.sharding import PartitionSpec as P

TILE = 512
K = 256
RMAX = 64


def broadcast(block, axis, holder):
    block = jnp.where(lax.axis_index(axis) == holder, block, jnp.zeros_like(block))
    return lax.psum(block, axis)


def local(omega, psi, near_tiles, left_factors, right_factors, admissible, ranks):
    tile_rows = admissible.shape[0]
    tile_cols = admissible.shape[1]
    row_place = lax.axis_index("row")
    col_place = lax.axis_index("col")
    whole = lax.all_gather(omega, "row", axis=0, tiled=True)
    columns = lax.dynamic_slice_in_dim(whole, col_place * tile_cols * TILE, tile_cols * TILE, 0)
    own_piece = lax.dynamic_slice_in_dim(psi, row_place % 2 * tile_rows * TILE, tile_rows * TILE, 0)
    psi_rows = broadcast(own_piece, "col", row_place // 2)
    ufac = left_factors.reshape(tile_rows, TILE, tile_cols, RMAX)
    vfac = right_factors.reshape(tile_rows, RMAX, tile_cols, TILE)
    omega_tiles = columns.reshape(tile_cols, TILE, K)
    psi_tiles = psi_rows.reshape(tile_rows, TILE, K)
    levels = jnp.arange(RMAX, dtype=jnp.int32)
    keep = ((levels[None, None, :] < ranks[:, :, None]) & (admissible[:, :, None] == 1)).astype(
        jnp.float32
    )
    coeff = jnp.einsum("arbt,btk->abrk", vfac, omega_tiles, preferred_element_type=jnp.float32)
    coeff = (coeff * keep[..., None]).astype(jnp.bfloat16)
    y_low = jnp.einsum("atbr,abrk->atk", ufac, coeff, preferred_element_type=jnp.float32)
    left_coeff = jnp.einsum("atbr,atk->abrk", ufac, psi_tiles, preferred_element_type=jnp.float32)
    left_coeff = (left_coeff * keep[..., None]).astype(jnp.bfloat16)
    z_low = jnp.einsum("arbt,abrk->btk", vfac, left_coeff, preferred_element_type=jnp.float32)
    y_part = y_low.reshape(tile_rows * TILE, K)
    z_part = z_low.reshape(tile_cols * TILE, K)

    def dense_tile(index, carry):
        upper = index // tile_cols
        lower = index % tile_cols
        offset = col_place * tile_cols + lower - (row_place * tile_rows + upper) + 1
        flag = (admissible[upper, lower] == 0) & (offset >= 0) & (offset <= 2)

        def take(sums):
            y_acc, z_acc = sums
            block = lax.dynamic_slice(
                near_tiles, (upper * TILE, jnp.clip(offset, 0, 2) * TILE), (TILE, TILE)
            )
            om_block = lax.dynamic_slice_in_dim(columns, lower * TILE, TILE, 0)
            ps_block = lax.dynamic_slice_in_dim(psi_rows, upper * TILE, TILE, 0)
            y_add = jnp.dot(block, om_block, preferred_element_type=jnp.float32)
            z_add = lax.dot_general(
                block, ps_block, (((0,), (0,)), ((), ())), preferred_element_type=jnp.float32
            )
            y_now = lax.dynamic_slice_in_dim(y_acc, upper * TILE, TILE, 0)
            z_now = lax.dynamic_slice_in_dim(z_acc, lower * TILE, TILE, 0)
            y_acc = lax.dynamic_update_slice_in_dim(y_acc, y_now + y_add, upper * TILE, 0)
            z_acc = lax.dynamic_update_slice_in_dim(z_acc, z_now + z_add, lower * TILE, 0)
            return (y_acc, z_acc)

        def leave(sums):
            return sums

        return lax.cond(flag, take, leave, carry)

    y_part, z_part = lax.fori_loop(0, tile_rows * tile_cols, dense_tile, (y_part, z_part))
    samples_right = lax.psum_scatter(y_part, "col", scatter_dimension=0, tiled=True)
    samples_left = lax.psum_scatter(z_part, "row", scatter_dimension=0, tiled=True)
    return (samples_right, samples_left)


def solution(mesh):
    return jax.shard_map(
        local,
        mesh=mesh,
        in_specs=(
            P("row", None),
            P("col", None),
            P("row", None),
            P("row", "col"),
            P("row", "col"),
            P("row", "col"),
            P("row", "col"),
        ),
        out_specs=(P(("row", "col"), None), P(("col", "row"), None)),
        check_vma=False,
    )
```

profile of v0, /device:TPU:16, one launch (start us, length us, event | category | flops | bytes accessed | tf_op | source)
XLA Modules:
  0.0 662.6 jit_solution(13030150450773221513)
XLA Ops:
  8.0 0.0 copy-start.5
  8.0 0.0 copy-start.6
  8.0 0.0 all-reduce.2.cloned.1.call-start
  8.1 2.0 dynamic-slice_select_fusion
  10.1 0.0 copy-start.7
  10.1 0.0 copy-start.8
  10.1 0.0 all-reduce.2.cloned.1.call-update
  10.1 0.0 all-gather.2.cloned.1.call-start
  10.2 0.5 all-gather.2.cloned.1.call-update
  10.7 0.0 reduce-scatter.3.cloned.1.call-start
  10.8 0.0 copy-done.5
  10.8 0.4 reshape.33
  11.1 0.0 copy-done.6
  11.2 0.0 copy-start.3
  11.2 0.2 copy.17
  11.4 0.4 reshape.34
  11.8 0.0 copy-done.7
  11.8 0.0 copy-start.4
  11.8 0.1 copy.15
  11.9 0.0 copy-done.8
  11.9 0.1 copy.14
  12.0 0.1 and_convert_fusion
  12.1 240.1 %all-reduce.2.cloned.1.call-done = bf16[1024,256]{1,0:T(8,128)(2,1)} async-done(((bf16[1024,256]{1,0:T(8,128)(2,1)}), bf16[1024,256]{1,0:T(8,128)(2,1)}) %all-reduce.2.cloned.1.call-update) | async-done | bytes 524304 | tf_op jit(solution)/shard_map/psum | solution.py:13
  252.1 0.0 copy-done.3
  252.1 0.0 copy-done.4
  252.1 3.2 convolution_bitcast_fusion
  255.3 1.9 copy.21
  257.2 0.0 all-gather.2.cloned.1.call-done
  257.2 1.3 constant_dynamic-slice_fusion
  258.5 0.0 copy-start.2
  258.6 1.0 copy-done.2
  259.5 2.9 convolution_bitcast_fusion.1
  262.4 1.6 copy.19
  264.0 10.7 %while.17 = (s32[]{:T(128)}, f32[1024,256]{1,0:T(8,128)S(1)}, f32[2048,256]{1,0:T(8,128)S(1)}, s32[2,4]{1,0:T(2,128)S(1)}, s32[]{:T(128)}, /*index=5*/s32[]{:T(1...) while((s32[]{:T(128)}, f32[1024,256]{1,0:T(8,128)S(1)}, ...), condition=%wide.region_4.5_spmd, body=%wide.region_1.4_spmd.sunk | while | flops 268697632 | bytes 3674816 | solution.py:70
  264.0 0.6 dynamic_slice.46
  265.3 0.6 dynamic_slice.46
  266.7 0.6 dynamic_slice.46
  268.0 0.6 dynamic_slice.46
  269.3 0.6 dynamic_slice.46
  270.7 0.6 dynamic_slice.46
  272.0 0.6 dynamic_slice.46
  273.4 0.6 dynamic_slice.46
  274.7 0.0 copy-start.1
  274.7 0.0 copy-start
  274.7 0.9 copy-done.1
  275.6 0.0 reduce-scatter.3.cloned.1.call-update
  275.7 0.0 reduce-scatter.5.cloned.1.call-start
  275.7 0.6 copy-done
  276.3 0.1 reduce-scatter.5.cloned.1.call-update
  276.4 229.9 %reduce-scatter.3.cloned.1.call-done = f32[64,256]{1,0:T(8,128)} async-done(((f32[1024,256]{1,0:T(8,128)}), f32[64,256]{1,0:T(8,128)}) %reduce-scatter.3.cloned.1.call-update) | async-done | bytes 65552 | tf_op jit(solution)/shard_map/reduce_scatter | solution.py:71
  506.4 149.1 %reduce-scatter.5.cloned.1.call-done = f32[64,256]{1,0:T(8,128)} async-done(((f32[2048,256]{1,0:T(8,128)}), f32[64,256]{1,0:T(8,128)}) %reduce-scatter.5.cloned.1.call-update) | async-done | bytes 65552 | tf_op jit(solution)/shard_map/reduce_scatter | solution.py:72
  (10 shorter events, 0.1 us)
Async XLA Ops:
  8.0 2.8 copy-start.5
  8.0 3.1 copy-start.6
  8.0 244.1 %all-reduce.2.cloned.1.call-start = ((), (), s32[]{:S(2)}) async-start(), calls=%async_computation.3 | async-start | bytes 1048576 | tf_op jit(solution)/shard_map/psum | solution.py:13
  10.1 1.7 copy-start.7
  10.1 1.8 copy-start.8
  10.1 247.1 %all-gather.2.cloned.1.call-start = ((), (), s32[]{:S(2)}) async-start(), calls=%async_computation.2 | async-start | bytes 17301504 | tf_op jit(solution)/shard_map/all_gather | solution.py:21
  10.7 495.7 %reduce-scatter.3.cloned.1.call-start = ((), (), s32[]{:S(2)}) async-start(), calls=%async_computation.4 | async-start | bytes 1114112 | tf_op jit(solution)/shard_map/reduce_scatter | solution.py:71
  11.2 241.0 %copy-start.3 = (bf16[2,64,4,512]{3,2,1,0:T(4,128)(2,1)}, bf16[2,64,4,512]{3,2,1,0:T(4,128)(2,1)S(1)}, u32[]{:S(2)}) copy-start(bf16[2,64,4,512]{3,2,1,0:T(4,128)(2,1)S(1)} %reshape.33) | copy-start | bytes 1572868
  11.8 240.4 %copy-start.4 = (bf16[2,512,4,64]{1,0,3,2:T(2,128)(2,1)}, bf16[2,512,4,64]{1,0,3,2:T(2,128)(2,1)S(1)}, u32[]{:S(2)}) copy-start(bf16[2,512,4,64]{1,0,3,2:T(2,128)(2,1)S(1)} %reshape.34) | copy-start | bytes 1572868
  258.5 1.0 copy-start.2
  274.7 1.0 copy-start.1
  274.7 1.6 copy-start
  275.7 379.8 %reduce-scatter.5.cloned.1.call-start = ((), (), s32[]{:S(2)}) async-start(), calls=%async_computation.5 | async-start | bytes 2162688 | tf_op jit(solution)/shard_map/reduce_scatter | solution.py:72
Sparse Core Ops, SparseCore 0:
  11.8 240.3 all-reduce.1
  275.8 230.5 reduce-scatter.2
  509.7 145.6 reduce-scatter.4
Sparse Core Ops, SparseCore 1:
  13.0 124.5 all-gather.1
where the time goes:
time: 663 us
  waiting for transfers between devices  620 us (94%)
  between operations  15.4 us (2%)
  local copies, waits for them, and re-layouts  13.6 us (2%)
    psum x1, waiting for transfers between devices, broadcast(): return lax.psum(block, axis)  240 us
    reduce_scatter x1, waiting for transfers between devices, local(): lax.psum_scatter(y_part, 'col', scatter_dimension=0, tiled=True)  230 us
    reduce_scatter x1, waiting for transfers between devices, local(): lax.psum_scatter(z_part, 'row', scatter_dimension=0, tiled=True)  149 us
  transfers between devices with their start and end apart: 4, of which 3 were waited for; matrix products, arithmetic and copies ran while one was open for 1% of the time, Pallas kernels for 0%

commit v1 on v0

v1 whole, which is shorter than its diff:
```python
import jax
import jax.numpy as jnp
from jax import lax
from jax.experimental import pallas as pl
from jax.experimental.pallas import tpu as pltpu
from jax.sharding import PartitionSpec as P

MESH = pl.DeviceIdType.MESH
TILE = 512
K = 256
RMAX = 64
F32 = jnp.float32
BF16 = jnp.bfloat16


def device(x, zl, k, y, zh):
    return (x * 8 + zl * 2 + k, y * 2 + zh)


def psi_source(z):
    return jnp.where(z == 4, 3, jnp.where(z == 3, 4, jnp.where(z == 6, 1, jnp.where(z == 1, 6, z))))


def parent(q, root):
    return jnp.where((root == 0) & (q == 3), 2, jnp.where((root == 3) & (q == 0), 1, root))


def kernel(omega, psi, near, left, right, adm, ranks, y_out, z_out,
           om, ps, nr, uu, vv, cr, cl, yp, y16, yr, yacc, yh, zp, zc, z16, zr,
           load_sem, ps_send, ps_recv, om_send, om_recv, tw_send, tw_recv,
           y_send, y_recv, h_send, h_recv, c_send, c_recv, z_send, z_recv):
    row = lax.axis_index("row")
    col = lax.axis_index("col")
    x, zl, k = row // 8, (row // 2) % 4, row % 2
    y, zh = col // 2, col % 2
    z = zh * 4 + zl
    place = row // 2

    xs, qs = y // 2, (y % 2) * 2 + zh
    ps_y = 2 * x + zl // 2
    ps_z = psi_source(z)
    tz = psi_source(z)
    tx = y // 2
    serves = (tz % 4) == (y % 2) * 2 + zh
    om_root = (x == xs) & (zl == qs)
    first = k == 0

    def remote(src, dst, ss, rs, dev):
        return pltpu.make_async_remote_copy(src_ref=src, dst_ref=dst, send_sem=ss, recv_sem=rs,
                                            device_id=dev, device_id_type=MESH)

    om_from_x = jnp.where(first, zl == qs, x != xs) & ~om_root
    om_from_z = jnp.where(first, zl != qs, (x == xs) & (zl != qs))
    sends_x = jnp.where(first, om_root, x == xs)
    may_send_z = jnp.where(first, True, x == xs)

    barrier = pltpu.get_barrier_semaphore()

    def greet(dev):
        pl.semaphore_signal(barrier, inc=1, device_id=dev, device_id_type=MESH)

    count = 0
    for i in range(4):
        mine = (x == i) & (y == ps_y) & (z == ps_z)

        @pl.when(jnp.logical_not(mine))
        def _(i=i):
            greet(device(i, ps_z % 4, k, ps_y, ps_z // 4))
    for i in range(8):
        other = serves & jnp.logical_not((x == tx) & (y == i) & (z == tz))
        count += jnp.where(other, 1, 0)

    @pl.when(om_from_x)
    def _():
        greet(device(xs, zl, k, y, zh))

    @pl.when(om_from_z)
    def _():
        greet(device(x, parent(zl, qs), k, y, zh))
    count += jnp.where(sends_x, 3, 0)
    for q in range(4):
        child = may_send_z & (q != qs) & (parent(q, qs) == zl)
        count += jnp.where(child, 1, 0)
    greet(device(x, zl, 1 - k, y, zh))
    for i in range(1, 8):
        greet(device(x, zl, k, (y + i) % 8, zh))
    greet(device(x, zl, k, y, 1 - zh))
    for i in range(1, 16):
        p = (place + i) % 16
        greet(device(p // 4, p % 4, k, y, zh))
    count += 1 + 7 + 1 + 15

    loads = [pltpu.make_async_copy(right, vv, load_sem.at[0]),
             pltpu.make_async_copy(left, uu, load_sem.at[1]),
             pltpu.make_async_copy(near, nr, load_sem.at[2])]
    for c in loads:
        c.start()
    pl.semaphore_wait(barrier, count)

    ps_sends = []
    for i in range(8):
        other = serves & jnp.logical_not((x == tx) & (y == i) & (z == tz))
        src = psi.at[pl.ds(pl.multiple_of(k * 1024 + x * 256, 256), 256)]
        dst = ps.at[pl.ds(pl.multiple_of(x * 256, 256), 256)]
        ps_sends.append((other, remote(src, dst, ps_send.at[i], ps_recv.at[x],
                                       device(tx, tz % 4, k, i, tz // 4))))
    own_psi = serves & (x == tx) & (z == tz)
    own_copy = pltpu.make_async_copy(psi.at[pl.ds(pl.multiple_of(k * 1024 + x * 256, 256), 256)],
                                     ps.at[pl.ds(pl.multiple_of(x * 256, 256), 256)], load_sem.at[3])

    slot = om.at[k]

    @pl.when(om_root)
    def _():
        c = pltpu.make_async_copy(omega, slot, load_sem.at[4])
        c.start()
        c.wait()

    for cond, c in ps_sends:
        @pl.when(cond)
        def _(c=c):
            c.start()

    @pl.when(own_psi)
    def _():
        own_copy.start()

    @pl.when(jnp.logical_not(om_root))
    def _():
        remote(slot, slot, om_send.at[0], om_recv, device(x, zl, 1 - k, y, zh)).wait_recv()

    om_sends = []
    for i in range(1, 4):
        om_sends.append((sends_x, remote(slot, slot, om_send.at[i - 1], om_recv,
                                         device((x + i) % 4, zl, k, y, zh))))
    for q in range(4):
        child = may_send_z & (q != qs) & (parent(q, qs) == zl)
        om_sends.append((child, remote(slot, slot, om_send.at[3 + q], om_recv, device(x, q, k, y, zh))))
    for cond, c in om_sends:
        @pl.when(cond)
        def _(c=c):
            c.start()
    twin = remote(slot, slot, tw_send, tw_recv, device(x, zl, 1 - k, y, zh))
    twin.start()

    for c in loads:
        c.wait()

    level = lax.broadcasted_iota(jnp.int32, (RMAX, K), 0)

    def limit(a, b):
        return jnp.where(adm[a, b] == 1, ranks[a, b], 0)

    def flag(a, b):
        return jnp.where(adm[a, b] == 0, 1.0, 0.0).astype(F32)

    for i in range(4):
        mine = (x == i) & own_psi

        @pl.when(jnp.logical_not(mine & (y == ps_y)))
        def _(i=i):
            part = ps.at[pl.ds(i * 256, 256)]
            remote(part, part, ps_send.at[0], ps_recv.at[i], device(x, zl, 1 - k, y, zh)).wait_recv()

    @pl.when(own_psi)
    def _():
        own_copy.wait()

    for a in range(2):
        full = lax.dot_general(uu[a * TILE:(a + 1) * TILE, :], ps[a * TILE:(a + 1) * TILE, :],
                               (((0,), (0,)), ((), ())), preferred_element_type=F32)
        for b in range(4):
            piece = full[b * RMAX:(b + 1) * RMAX]
            cl[b, a * RMAX:(a + 1) * RMAX, :] = jnp.where(level < limit(a, b), piece, 0.0).astype(BF16)
    core_sends = []
    for b in range(4):
        part = lax.dot_general(vv[:, b * TILE:(b + 1) * TILE], cl[b], (((0,), (0,)), ((), ())),
                               preferred_element_type=F32)
        zp[4 * b:4 * b + 4] = part.reshape(4, 2, 64, K)
        for a in range(2):
            off = 4 * col + b - (2 * row + a) + 1

            @pl.when((off >= 0) & (off <= 2))
            def _(a=a, b=b, off=off):
                block = nr[a * TILE:(a + 1) * TILE, pl.ds(pl.multiple_of(off * TILE, TILE), TILE)]
                add = lax.dot_general(block, ps[a * TILE:(a + 1) * TILE, :], (((0,), (0,)), ((), ())),
                                      preferred_element_type=F32)
                zp[4 * b:4 * b + 4] += (add * flag(a, b)).reshape(4, 2, 64, K)
        c = remote(zp.at[pl.ds(4 * b, 4), 1 - k], zc.at[pl.ds(4 * b, 4)], c_send.at[b], c_recv.at[b],
                   device(x, zl, 1 - k, y, zh))
        c.start()
        core_sends.append(c)
    for b in range(4):
        core_sends[b].wait_recv()
        zc[4 * b:4 * b + 4] = zc[4 * b:4 * b + 4] + zp[4 * b:4 * b + 4, k]
        z16[4 * b:4 * b + 4] = zc[4 * b:4 * b + 4].astype(BF16)
    z_sends = []
    for i in range(1, 16):
        p = (place + i) % 16
        c = remote(z16.at[p], zr.at[place], z_send.at[i], z_recv.at[place], device(p // 4, p % 4, k, y, zh))
        c.start()
        z_sends.append(c)

    twin.wait_recv()
    for b in range(4):
        half = om.at[b // 2]
        full = jnp.dot(vv[:, b * TILE:(b + 1) * TILE], half[(b % 2) * TILE:(b % 2 + 1) * TILE, :],
                       preferred_element_type=F32)
        for a in range(2):
            piece = full[a * RMAX:(a + 1) * RMAX]
            cr[a, b * RMAX:(b + 1) * RMAX, :] = jnp.where(level < limit(a, b), piece, 0.0).astype(BF16)
    y_sends = []
    for a in range(2):
        yp[4 * a:4 * a + 4] = jnp.dot(uu[a * TILE:(a + 1) * TILE, :], cr[a],
                                      preferred_element_type=F32).reshape(4, 128, K)
        for b in range(4):
            off = 4 * col + b - (2 * row + a) + 1

            @pl.when((off >= 0) & (off <= 2))
            def _(a=a, b=b, off=off):
                block = nr[a * TILE:(a + 1) * TILE, pl.ds(pl.multiple_of(off * TILE, TILE), TILE)]
                add = jnp.dot(block, om[b // 2, (b % 2) * TILE:(b % 2 + 1) * TILE, :],
                              preferred_element_type=F32)
                yp[4 * a:4 * a + 4] += (add * flag(a, b)).reshape(4, 128, K)
        y16[4 * a:4 * a + 4] = yp[4 * a:4 * a + 4].astype(BF16)
    for i in range(1, 8):
        p = (y + i) % 8
        c = remote(y16.at[p], yr.at[y], y_send.at[i], y_recv.at[y], device(x, zl, k, p, zh))
        c.start()
        y_sends.append(c)

    total = yp[y]
    for i in range(1, 8):
        p = (y + i) % 8
        remote(y16.at[p], yr.at[p], y_send.at[i], y_recv.at[p], device(x, zl, k, p, zh)).wait_recv()
        total += yr[p].astype(F32)
    yacc[...] = total.reshape(2, 64, K)
    across = remote(yacc.at[1 - zh], yh, h_send, h_recv, device(x, zl, k, y, 1 - zh))
    across.start()

    ztot = zc[place]
    for i in range(1, 16):
        p = (place + i) % 16
        remote(z16.at[p], zr.at[p], z_send.at[i], z_recv.at[p], device(p // 4, p % 4, k, y, zh)).wait_recv()
        ztot += zr[p].astype(F32)
    z_out[...] = ztot

    across.wait_recv()
    y_out[...] = yacc[zh] + yh[...]

    for cond, c in ps_sends + om_sends:
        @pl.when(cond)
        def _(c=c):
            c.wait_send()
    twin.wait_send()
    across.wait_send()
    for c in core_sends + z_sends + y_sends:
        c.wait_send()


def local(omega, psi, near_tiles, left_factors, right_factors, admissible, ranks):
    dma = pltpu.SemaphoreType.DMA
    anywhere = pl.BlockSpec(memory_space=pl.ANY)
    scalars = pl.BlockSpec(memory_space=pltpu.SMEM)
    vmem = pl.BlockSpec(memory_space=pltpu.VMEM)
    out = jax.ShapeDtypeStruct((64, K), F32)
    return pl.pallas_call(
        kernel,
        out_shape=(out, out),
        in_specs=[anywhere] * 5 + [scalars] * 2,
        out_specs=(vmem, vmem),
        scratch_shapes=[
            pltpu.VMEM((2, 1024, K), BF16),
            pltpu.VMEM((1024, K), BF16),
            pltpu.VMEM((1024, 3 * TILE), BF16),
            pltpu.VMEM((1024, 256), BF16),
            pltpu.VMEM((128, 2048), BF16),
            pltpu.VMEM((2, 256, K), BF16),
            pltpu.VMEM((4, 128, K), BF16),
            pltpu.VMEM((8, 128, K), F32),
            pltpu.VMEM((8, 128, K), BF16),
            pltpu.VMEM((8, 128, K), BF16),
            pltpu.VMEM((2, 64, K), F32),
            pltpu.VMEM((64, K), F32),
            pltpu.VMEM((16, 2, 64, K), F32),
            pltpu.VMEM((16, 64, K), F32),
            pltpu.VMEM((16, 64, K), BF16),
            pltpu.VMEM((16, 64, K), BF16),
            dma((5,)), dma((8,)), dma((4,)), dma((7,)), dma, dma, dma,
            dma((8,)), dma((8,)), dma, dma, dma((4,)), dma((4,)), dma((16,)), dma((16,)),
        ],
        compiler_params=pltpu.CompilerParams(collective_id=0, has_side_effects=True,
                                             vmem_limit_bytes=48 << 20),
        cost_estimate=pl.CostEstimate(flops=2 * 10 ** 9, bytes_accessed=6 << 20, transcendentals=0),
    )(omega, psi, near_tiles, left_factors, right_factors, admissible, ranks)


def solution(mesh):
    return jax.shard_map(
        local,
        mesh=mesh,
        in_specs=(
            P("row", None),
            P("col", None),
            P("row", None),
            P("row", "col"),
            P("row", "col"),
            P("row", "col"),
            P("row", "col"),
        ),
        out_specs=(P(("row", "col"), None), P(("col", "row"), None)),
        check_vma=False,
    )
```

time: 663 us -> 106 us (0.16)
  the two profiles are of different devices: /device:TPU:16 before, /device:TPU:192 now
where the time goes in v1:
time: 106 us; the launch traced here: 105 us
  Pallas kernels  95.7 us (90%)
  local copies, waits for them, and re-layouts  8.85 us (8%)
    pallas_call x1, Pallas kernels, local(): pl.pallas_call(kernel, out_shape=(out, out), in_specs=[anywhere] * 5 + [s...  95.7 us
    unnamed x16, local copies, waits for them, and re-layouts  8.85 us

profile of v1, /device:TPU:192, one launch (start us, length us, event | category | flops | bytes accessed | tf_op | source)
XLA Modules:
  0.0 105.2 jit_solution(14848926912168459962)
XLA Ops:
  0.6 0.0 copy-start
  0.6 1.9 %copy-done = bf16[1024,1536]{1,0:T(8,128)(2,1)S(1)} copy-done((bf16[1024,1536]{1,0:T(8,128)(2,1)S(1)}, bf16[1024,1536]{1,0:T(8,128)(2,1)}, u32[]{:S(2)}) %copy-start) | copy-done | bytes 3145752
  2.5 0.0 copy-start.1
  2.5 1.2 %copy-done.1 = bf16[2048,256]{1,0:T(8,128)(2,1)S(1)} copy-done((bf16[2048,256]{1,0:T(8,128)(2,1)S(1)}, bf16[2048,256]{1,0:T(8,128)(2,1)}, u32[]{:S(2)}) %copy-start.1) | copy-done | bytes 1048600
  3.7 0.0 copy-start.2
  3.8 1.0 copy-done.2
  4.8 0.0 copy-start.3
  4.8 1.0 copy-done.3
  5.8 0.0 copy-start.4
  5.8 1.0 copy-done.4
  6.9 0.0 copy-start.5
  6.9 0.7 copy-done.5
  7.6 0.0 copy-start.6
  7.6 0.7 copy-done.6
  8.2 95.7 %shard_map.86 = (f32[64,256]{1,0:T(8,128)S(1)}, f32[64,256]{1,0:T(8,128)S(1)}) custom-call(bf16[1024,256]{1,0:T(8,128)(2,1)S(1)} %copy-done.2, bf16[2048,256]{1,0:T(8,128)(2,1)S(1)} %copy-done.1, bf16[1024,1536]{1,0:T(8,128)(2,1)S(1)} %copy-done, bf16[1024,256]{1,0:T(8,128)(2,1)S(1)} %copy-done.3, bf16[128,2048]{1,0:T(8,128)(2,1)S(1)} %copy-done.4, ...), custom_call_target="tpu_custom_call" | custom-call | flops 2000000000 | bytes 6291456 | tf_op jit(solution)/shard_map/pallas_call | solution.py:267
  103.9 0.6 copy.11
  104.6 0.6 copy.12
Async XLA Ops:
  0.6 1.9 %copy-start = (bf16[1024,1536]{1,0:T(8,128)(2,1)S(1)}, bf16[1024,1536]{1,0:T(8,128)(2,1)}, u32[]{:S(2)}) copy-start(bf16[1024,1536]{1,0:T(8,128)(2,1)} %near.1) | copy-start | bytes 9437188
  2.5 1.2 %copy-start.1 = (bf16[2048,256]{1,0:T(8,128)(2,1)S(1)}, bf16[2048,256]{1,0:T(8,128)(2,1)}, u32[]{:S(2)}) copy-start(bf16[2048,256]{1,0:T(8,128)(2,1)} %psi.1) | copy-start | bytes 3145732
  3.7 1.0 copy-start.2
  4.8 1.0 copy-start.3
  5.8 1.0 copy-start.4
  6.9 0.7 copy-start.5
  7.6 0.7 copy-start.6

commit v2 on v1

--- a/solution.py
+++ b/solution.py
@@ -21,13 +21,9 @@
     return jnp.where(z == 4, 3, jnp.where(z == 3, 4, jnp.where(z == 6, 1, jnp.where(z == 1, 6, z))))
 
 
-def parent(q, root):
-    return jnp.where((root == 0) & (q == 3), 2, jnp.where((root == 3) & (q == 0), 1, root))
-
-
-def kernel(omega, psi, near, left, right, adm, ranks, y_out, z_out,
+def kernel(omega, psi, near, left, right, adm_in, ranks_in, y_out, z_out,
            om, ps, nr, uu, vv, cr, cl, yp, y16, yr, yacc, yh, zp, zc, z16, zr,
-           load_sem, ps_send, ps_recv, om_send, om_recv, tw_send, tw_recv,
+           adm, ranks, load_sem, ps_send, ps_recv, om_send, om_recv, tw_send, tw_recv,
            y_send, y_recv, h_send, h_recv, c_send, c_recv, z_send, z_recv):
     row = lax.axis_index("row")
     col = lax.axis_index("col")
@@ -49,10 +45,12 @@
         return pltpu.make_async_remote_copy(src_ref=src, dst_ref=dst, send_sem=ss, recv_sem=rs,
                                             device_id=dev, device_id_type=MESH)
 
-    om_from_x = jnp.where(first, zl == qs, x != xs) & ~om_root
-    om_from_z = jnp.where(first, zl != qs, (x == xs) & (zl != qs))
-    sends_x = jnp.where(first, om_root, x == xs)
-    may_send_z = jnp.where(first, True, x == xs)
+    u, v = jnp.where(first, x, zl), jnp.where(first, zl, x)
+    us, vs = jnp.where(first, xs, qs), jnp.where(first, qs, xs)
+    on_axis = v == vs
+
+    def at(a, b):
+        return device(jnp.where(first, a, b), jnp.where(first, b, a), k, y, zh)
 
     barrier = pltpu.get_barrier_semaphore()
 
@@ -70,17 +68,20 @@
         other = serves & jnp.logical_not((x == tx) & (y == i) & (z == tz))
         count += jnp.where(other, 1, 0)
 
-    @pl.when(om_from_x)
-    def _():
-        greet(device(xs, zl, k, y, zh))
-
-    @pl.when(om_from_z)
-    def _():
-        greet(device(x, parent(zl, qs), k, y, zh))
-    count += jnp.where(sends_x, 3, 0)
-    for q in range(4):
-        child = may_send_z & (q != qs) & (parent(q, qs) == zl)
-        count += jnp.where(child, 1, 0)
+    @pl.when(on_axis & (u != us))
+    def _():
+        greet(at(us, vs))
+
+    @pl.when(jnp.logical_not(on_axis))
+    def _():
+        greet(at(u, vs))
+
+    @pl.when(jnp.logical_not(om_root))
+    def _():
+        for i in range(1, 4):
+            greet(at((u + i) % 4, v))
+    count += jnp.where(om_root, 3, 0) + jnp.where(on_axis, 3, 0)
+    count += jnp.where(on_axis & (u != us), 2, 3)
     greet(device(x, zl, 1 - k, y, zh))
     for i in range(1, 8):
         greet(device(x, zl, k, (y + i) % 8, zh))
@@ -92,10 +93,21 @@
 
     loads = [pltpu.make_async_copy(right, vv, load_sem.at[0]),
              pltpu.make_async_copy(left, uu, load_sem.at[1]),
-             pltpu.make_async_copy(near, nr, load_sem.at[2])]
+             pltpu.make_async_copy(near, nr, load_sem.at[2]),
+             pltpu.make_async_copy(adm_in, adm, load_sem.at[5]),
+             pltpu.make_async_copy(ranks_in, ranks, load_sem.at[6])]
+    root_copy = pltpu.make_async_copy(omega, om.at[k], load_sem.at[4])
+
+    @pl.when(om_root)
+    def _():
+        root_copy.start()
     for c in loads:
         c.start()
     pl.semaphore_wait(barrier, count)
+
+    @pl.when(om_root)
+    def _():
+        root_copy.wait()
 
     ps_sends = []
     for i in range(8):
@@ -110,11 +122,8 @@
 
     slot = om.at[k]
 
-    @pl.when(om_root)
-    def _():
-        c = pltpu.make_async_copy(omega, slot, load_sem.at[4])
-        c.start()
-        c.wait()
+    def quarter(j):
+        return slot.at[pl.ds(pl.multiple_of(j * 256, 256), 256)]
 
     for cond, c in ps_sends:
         @pl.when(cond)
@@ -125,23 +134,41 @@
     def _():
         own_copy.start()
 
+    om_sends = []
+
+    def send_omega(cond, j, sem, dev):
+        c = remote(quarter(j), quarter(j), om_send.at[sem], om_recv.at[j], dev)
+        om_sends.append((cond, c))
+
+        @pl.when(cond)
+        def _():
+            c.start()
+
+    def omega_arrived(j):
+        remote(quarter(j), quarter(j), om_send.at[0], om_recv.at[j], device(x, zl, 1 - k, y, zh)).wait_recv()
+
+    for i in range(1, 4):
+        j = (us + i) % 4
+        send_omega(om_root, j, i - 1, at(j, vs))
+
     @pl.when(jnp.logical_not(om_root))
     def _():
-        remote(slot, slot, om_send.at[0], om_recv, device(x, zl, 1 - k, y, zh)).wait_recv()
-
-    om_sends = []
+        omega_arrived(u)
     for i in range(1, 4):
-        om_sends.append((sends_x, remote(slot, slot, om_send.at[i - 1], om_recv,
-                                         device((x + i) % 4, zl, k, y, zh))))
-    for q in range(4):
-        child = may_send_z & (q != qs) & (parent(q, qs) == zl)
-        om_sends.append((child, remote(slot, slot, om_send.at[3 + q], om_recv, device(x, q, k, y, zh))))
-    for cond, c in om_sends:
-        @pl.when(cond)
-        def _(c=c):
-            c.start()
-    twin = remote(slot, slot, tw_send, tw_recv, device(x, zl, 1 - k, y, zh))
-    twin.start()
+        send_omega(on_axis, u, 2 + i, at(u, (v + i) % 4))
+    for i in range(1, 4):
+        j = (u + i) % 4
+        send_omega(jnp.logical_not(on_axis & (j == us)), u, 5 + i, at(j, v))
+    twins = []
+    for i in range(4):
+        j = (u + i) % 4
+        if i:
+            @pl.when(jnp.logical_not(om_root))
+            def _(j=j):
+                omega_arrived(j)
+        c = remote(quarter(j), quarter(j), tw_send.at[j], tw_recv.at[j], device(x, zl, 1 - k, y, zh))
+        c.start()
+        twins.append(c)
 
     for c in loads:
         c.wait()
@@ -201,7 +228,10 @@
         c.start()
         z_sends.append(c)
 
-    twin.wait_recv()
+    other_half = om.at[1 - k]
+    for j in range(4):
+        part = other_half.at[pl.ds(256 * j, 256)]
+        remote(part, part, tw_send.at[j], tw_recv.at[j], device(x, zl, 1 - k, y, zh)).wait_recv()
     for b in range(4):
         half = om.at[b // 2]
         full = jnp.dot(vv[:, b * TILE:(b + 1) * TILE], half[(b % 2) * TILE:(b % 2 + 1) * TILE, :],
@@ -252,22 +282,20 @@
         @pl.when(cond)
         def _(c=c):
             c.wait_send()
-    twin.wait_send()
     across.wait_send()
-    for c in core_sends + z_sends + y_sends:
+    for c in twins + core_sends + z_sends + y_sends:
         c.wait_send()
 
 
 def local(omega, psi, near_tiles, left_factors, right_factors, admissible, ranks):
     dma = pltpu.SemaphoreType.DMA
     anywhere = pl.BlockSpec(memory_space=pl.ANY)
-    scalars = pl.BlockSpec(memory_space=pltpu.SMEM)
     vmem = pl.BlockSpec(memory_space=pltpu.VMEM)
     out = jax.ShapeDtypeStruct((64, K), F32)
     return pl.pallas_call(
         kernel,
         out_shape=(out, out),
-        in_specs=[anywhere] * 5 + [scalars] * 2,
+        in_specs=[anywhere] * 7,
         out_specs=(vmem, vmem),
         scratch_shapes=[
             pltpu.VMEM((2, 1024, K), BF16),
@@ -286,11 +314,13 @@
             pltpu.VMEM((16, 64, K), F32),
             pltpu.VMEM((16, 64, K), BF16),
             pltpu.VMEM((16, 64, K), BF16),
-            dma((5,)), dma((8,)), dma((4,)), dma((7,)), dma, dma, dma,
+            pltpu.SMEM((2, 4), jnp.int32),
+            pltpu.SMEM((2, 4), jnp.int32),
+            dma((7,)), dma((8,)), dma((4,)), dma((9,)), dma((4,)), dma((4,)), dma((4,)),
             dma((8,)), dma((8,)), dma, dma, dma((4,)), dma((4,)), dma((16,)), dma((16,)),
         ],
         compiler_params=pltpu.CompilerParams(collective_id=0, has_side_effects=True,
-                                             vmem_limit_bytes=48 << 20),
+                                             vmem_limit_bytes=64 << 20),
         cost_estimate=pl.CostEstimate(flops=2 * 10 ** 9, bytes_accessed=6 << 20, transcendentals=0),
     )(omega, psi, near_tiles, left_factors, right_factors, admissible, ranks)
 

time: 106 us -> 70.4 us (0.66)
  the two profiles are of different devices: /device:TPU:192 before, /device:TPU:144 now
where the time goes in v2:
time: 70.4 us; the launch traced here: 70.2 us
  Pallas kernels  66.7 us (95%)
  local copies, waits for them, and re-layouts  2.95 us (4%)
    pallas_call x1, Pallas kernels, local(): pl.pallas_call(kernel, out_shape=(out, out), in_specs=[anywhere] * 7, out...  66.7 us
    unnamed x2, local copies, waits for them, and re-layouts  2.95 us

profile of v2, /device:TPU:144, one launch (start us, length us, event | category | flops | bytes accessed | tf_op | source)
XLA Modules:
  0.0 70.2 jit_solution(9138068673350651692)
XLA Ops:
  0.6 66.7 %shard_map.86 = (f32[64,256]{1,0:T(8,128)}, f32[64,256]{1,0:T(8,128)}) custom-call(bf16[1024,256]{1,0:T(8,128)(2,1)} %omega.1, bf16[2048,256]{1,0:T(8,128)(2,1)} %psi.1, bf16[1024,1536]{1,0:T(8,128)(2,1)} %near.1, bf16[1024,256]{1,0:T(8,128)(2,1)} %left.1, bf16[128,2048]{1,0:T(8,128)(2,1)} %right.1, s32[2,4]{1,0:T(2,128)} %adm_in.1, s32[2,4]{1,0:T(2,128)} %ranks_in.1), custom_call_target="tpu_custom_call" | custom-call | flops 2000000000 | bytes 6291456 | tf_op jit(solution)/shard_map/pallas_call | solution.py:295
  67.3 1.5 %copy.11 = f32[64,256]{1,0:T(8,128)} copy(f32[64,256]{1,0:T(8,128)} %get-tuple-element.4) | data formatting | bytes 131072
  68.8 1.5 %copy.12 = f32[64,256]{1,0:T(8,128)} copy(f32[64,256]{1,0:T(8,128)} %get-tuple-element.5) | data formatting | bytes 131072

commit v3 on v0

v3 whole, which is shorter than its diff:
```python
import jax
import jax.numpy as jnp
from jax import lax
from jax.experimental import pallas as pl
from jax.experimental.pallas import tpu as pltpu
from jax.sharding import PartitionSpec as P

MESH = pl.DeviceIdType.MESH
TILE = 512
K = 256
KH = 128
RMAX = 64
F32 = jnp.float32
BF16 = jnp.bfloat16


def device(x, zl, k, y, zh):
    return (x * 8 + zl * 2 + k, y * 2 + zh)


def relay_source(z):
    return jnp.where(z == 4, 3, jnp.where(z == 3, 4, jnp.where(z == 6, 0, 7)))


def kernel(omega, psi, near, left, right, adm_in, ranks_in, y_out, z_out,
           om, ps, pr, nr, uu, vv, cr, cl, yp, y16, yr, yacc, yh, zp, zc, z16, zr,
           adm, ranks, load_sem, pr_send, pr_recv, ps_send, ps_recv, om_send, om_recv, tw_send, tw_recv,
           y_send, y_recv, h_send, h_recv, c_send, c_recv, z_send, z_recv):
    row = lax.axis_index("row")
    col = lax.axis_index("col")
    x, zl, k = row // 8, (row // 2) % 4, row % 2
    y, zh = col // 2, col % 2
    z = zh * 4 + zl
    place = row // 2

    xs, qs = y // 2, (y % 2) * 2 + zh
    ps_y = 2 * x + zl // 2
    tx = y // 2
    serves = (y % 2) == (zl // 2)
    holds = zh == zl % 2
    own_psi = serves & (x == tx)
    relayed = serves & jnp.logical_not(holds)
    rz = relay_source(z)
    tz = jnp.where(z == 3, 4, jnp.where(z == 4, 3, jnp.where(z == 0, 6, 1)))
    relays = jnp.where((z == 3) | (z == 7), y % 2 == 0, ((z == 4) | (z == 0)) & (y % 2 == 1))
    om_root = (x == xs) & (zl == qs)
    first = k == 0

    def remote(src, dst, ss, rs, dev):
        return pltpu.make_async_remote_copy(src_ref=src, dst_ref=dst, send_sem=ss, recv_sem=rs,
                                            device_id=dev, device_id_type=MESH)

    u, v = jnp.where(first, x, zl), jnp.where(first, zl, x)
    us, vs = jnp.where(first, xs, qs), jnp.where(first, qs, xs)
    on_axis = v == vs

    def at(a, b):
        return device(jnp.where(first, a, b), jnp.where(first, b, a), k, y, zh)

    barrier = pltpu.get_barrier_semaphore()

    def greet(dev):
        pl.semaphore_signal(barrier, inc=1, device_id=dev, device_id_type=MESH)

    count = 0
    for i in range(4):
        @pl.when(jnp.logical_not(own_psi & (x == i)))
        def _(i=i):
            greet(device(i, zl, k, ps_y, zh))

    @pl.when(relayed)
    def _():
        greet(device(x, rz % 4, k, y, rz // 4))
    count += jnp.where(relays, 1, 0) + jnp.where(serves, jnp.where(x == tx, 7, 8), 0)

    @pl.when(on_axis & (u != us))
    def _():
        greet(at(us, vs))

    @pl.when(jnp.logical_not(on_axis))
    def _():
        greet(at(u, vs))

    @pl.when(jnp.logical_not(om_root))
    def _():
        for i in range(1, 4):
            greet(at((u + i) % 4, v))
    count += jnp.where(om_root, 3, 0) + jnp.where(on_axis, 3, 0)
    count += jnp.where(on_axis & (u != us), 2, 3)
    greet(device(x, zl, 1 - k, y, zh))
    for i in range(1, 8):
        greet(device(x, zl, k, (y + i) % 8, zh))
    greet(device(x, zl, k, y, 1 - zh))
    for i in range(1, 16):
        p = (place + i) % 16
        greet(device(p // 4, p % 4, k, y, zh))
    count += 1 + 7 + 1 + 15

    loads = [pltpu.make_async_copy(right, vv, load_sem.at[0]),
             pltpu.make_async_copy(left, uu, load_sem.at[1]),
             pltpu.make_async_copy(near, nr, load_sem.at[2]),
             pltpu.make_async_copy(adm_in, adm, load_sem.at[3]),
             pltpu.make_async_copy(ranks_in, ranks, load_sem.at[4])]
    root_copies = [pltpu.make_async_copy(omega.at[:, pl.ds(h * KH, KH)], om.at[k, h], load_sem.at[5 + h])
                   for h in range(2)]

    @pl.when(om_root)
    def _():
        for c in root_copies:
            c.start()
    for c in loads:
        c.start()
    pl.semaphore_wait(barrier, count)

    @pl.when(om_root)
    def _():
        for c in root_copies:
            c.wait()

    sibling = device(x, zl, 1 - k, y, zh)
    my_quarter = pl.ds(pl.multiple_of(x * 256, 256), 256)
    pending = []

    def start(cond, c):
        pending.append((cond, c))
        if cond is None:
            c.start()
        else:
            @pl.when(cond)
            def _():
                c.start()

    def arrived(buf, sem):
        remote(buf, buf, c_send.at[0, 0], sem, sibling).wait_recv()

    def psi_part(h):
        return psi.at[pl.ds(pl.multiple_of(k * 1024 + x * 256, 256), 256), pl.ds(h * KH, KH)]

    def relay_psi(h):
        start(relays, remote(psi_part(h), pr.at[h], pr_send.at[h], pr_recv.at[h],
                             device(x, tz % 4, k, y, tz // 4)))

    def own_psi_copy(h, src):
        return pltpu.make_async_copy(src, ps.at[h, my_quarter], load_sem.at[7 + h])

    def send_psi(h, relay):
        cond = serves & (relayed if relay else holds)
        src = pr.at[h] if relay else psi_part(h)
        if relay:
            @pl.when(cond)
            def _():
                arrived(pr.at[h], pr_recv.at[h])
        for i in range(8):
            start(cond & jnp.logical_not((x == tx) & (y == i)),
                  remote(src, ps.at[h, my_quarter], ps_send.at[h, i], ps_recv.at[h, x], device(tx, zl, k, i, zh)))

        @pl.when(cond & (x == tx))
        def _():
            own_psi_copy(h, src).start()

    def psi_arrived(h):
        for i in range(4):
            @pl.when(jnp.logical_not(own_psi & (x == i)))
            def _(i=i):
                arrived(ps.at[h, pl.ds(i * 256, 256)], ps_recv.at[h, i])

        @pl.when(own_psi)
        def _():
            own_psi_copy(h, pr.at[h]).wait()

    def quarter(h, j):
        return om.at[k, h, pl.ds(pl.multiple_of(j * 256, 256), 256)]

    def send_omega(h, cond, j, sem, dev):
        start(cond, remote(quarter(h, j), quarter(h, j), om_send.at[h, sem], om_recv.at[h, j], dev))

    def scatter_omega(h):
        for i in range(1, 4):
            j = (us + i) % 4
            send_omega(h, om_root, j, i - 1, at(j, vs))

    def spread_omega(h):
        @pl.when(jnp.logical_not(om_root))
        def _():
            arrived(quarter(h, u), om_recv.at[h, u])
        for i in range(1, 4):
            send_omega(h, on_axis, u, 2 + i, at(u, (v + i) % 4))
        for i in range(1, 4):
            j = (u + i) % 4
            send_omega(h, jnp.logical_not(on_axis & (j == us)), u, 5 + i, at(j, v))

    def share_omega(h):
        for i in range(4):
            j = (u + i) % 4
            if i:
                @pl.when(jnp.logical_not(om_root))
                def _(j=j):
                    arrived(quarter(h, j), om_recv.at[h, j])
            start(None, remote(quarter(h, j), quarter(h, j), tw_send.at[h, j], tw_recv.at[h, j], sibling))

    def omega_arrived(h):
        for j in range(4):
            arrived(om.at[1 - k, h, pl.ds(256 * j, 256)], tw_recv.at[h, j])

    level = lax.broadcasted_iota(jnp.int32, (RMAX, KH), 0)

    def limit(a, b):
        return jnp.where(adm[a, b] == 1, ranks[a, b], 0)

    def flag(a, b):
        return jnp.where(adm[a, b] == 0, 1.0, 0.0).astype(F32)

    def dense(a, b, add):
        off = 4 * col + b - (2 * row + a) + 1

        @pl.when((off >= 0) & (off <= 2))
        def _():
            add(nr[a * TILE:(a + 1) * TILE, pl.ds(pl.multiple_of(off * TILE, TILE), TILE)])

    def left_products(h):
        for a in range(2):
            full = lax.dot_general(uu[a * TILE:(a + 1) * TILE, :], ps[h, a * TILE:(a + 1) * TILE, :],
                                   (((0,), (0,)), ((), ())), preferred_element_type=F32)
            for b in range(4):
                piece = full[b * RMAX:(b + 1) * RMAX]
                cl[b, a * RMAX:(a + 1) * RMAX, :] = jnp.where(level < limit(a, b), piece, 0.0).astype(BF16)
        for b in range(4):
            part = lax.dot_general(vv[:, b * TILE:(b + 1) * TILE], cl[b], (((0,), (0,)), ((), ())),
                                   preferred_element_type=F32)
            zp[h, 4 * b:4 * b + 4] = part.reshape(4, 2, 64, KH)
            for a in range(2):
                def add(block, a=a, b=b):
                    more = lax.dot_general(block, ps[h, a * TILE:(a + 1) * TILE, :], (((0,), (0,)), ((), ())),
                                           preferred_element_type=F32)
                    zp[h, 4 * b:4 * b + 4] += (more * flag(a, b)).reshape(4, 2, 64, KH)
                dense(a, b, add)
            start(None, remote(zp.at[h, pl.ds(4 * b, 4), 1 - k], zc.at[h, pl.ds(4 * b, 4)], c_send.at[h, b],
                               c_recv.at[h, b], sibling))

    def send_left(h):
        for b in range(4):
            arrived(zc.at[h, pl.ds(4 * b, 4)], c_recv.at[h, b])
            both = zc[h, 4 * b:4 * b + 4] + zp[h, 4 * b:4 * b + 4, k]
            zc[h, 4 * b:4 * b + 4] = both
            z16[h, 4 * b:4 * b + 4] = both.astype(BF16)
        for i in range(1, 16):
            p = (place + i) % 16
            start(None, remote(z16.at[h, p], zr.at[h, place], z_send.at[h, i], z_recv.at[h, place],
                               device(p // 4, p % 4, k, y, zh)))

    def sum_left(h):
        total = zc[h, place]
        for i in range(1, 16):
            p = (place + i) % 16
            arrived(zr.at[h, p], z_recv.at[h, p])
            total += zr[h, p].astype(F32)
        z_out[:, h * KH:(h + 1) * KH] = total

    def right_products(h):
        for b in range(4):
            full = jnp.dot(vv[:, b * TILE:(b + 1) * TILE], om[b // 2, h, (b % 2) * TILE:(b % 2 + 1) * TILE, :],
                           preferred_element_type=F32)
            for a in range(2):
                piece = full[a * RMAX:(a + 1) * RMAX]
                cr[a, b * RMAX:(b + 1) * RMAX, :] = jnp.where(level < limit(a, b), piece, 0.0).astype(BF16)
        for a in range(2):
            yp[h, 4 * a:4 * a + 4] = jnp.dot(uu[a * TILE:(a + 1) * TILE, :], cr[a],
                                             preferred_element_type=F32).reshape(4, 2, 64, KH)
            for b in range(4):
                def add(block, a=a, b=b):
                    more = jnp.dot(block, om[b // 2, h, (b % 2) * TILE:(b % 2 + 1) * TILE, :],
                                   preferred_element_type=F32)
                    yp[h, 4 * a:4 * a + 4] += (more * flag(a, b)).reshape(4, 2, 64, KH)
                dense(a, b, add)
            y16[h, 4 * a:4 * a + 4] = yp[h, 4 * a:4 * a + 4].astype(BF16)

    def send_right(h):
        for part in (1 - zh, zh):
            for i in range(1, 8):
                p = (y + i) % 8
                start(None, remote(y16.at[h, p, part], yr.at[h, y, part], y_send.at[h, part, i],
                                   y_recv.at[h, part, y], device(x, zl, k, p, zh)))

    def sum_right(h, part):
        total = yp[h, y, part]
        for i in range(1, 8):
            p = (y + i) % 8
            arrived(yr.at[h, p, part], y_recv.at[h, part, p])
            total += yr[h, p, part].astype(F32)
        return total

    def pass_right(h):
        yacc[h] = sum_right(h, 1 - zh)
        start(None, remote(yacc.at[h], yh.at[h], h_send.at[h], h_recv.at[h], device(x, zl, k, y, 1 - zh)))

    def end_right(h):
        total = sum_right(h, zh)
        arrived(yh.at[h], h_recv.at[h])
        y_out[:, h * KH:(h + 1) * KH] = total + yh[h]

    relay_psi(0)
    relay_psi(1)
    scatter_omega(0)
    send_psi(0, False)
    scatter_omega(1)
    send_psi(1, False)
    send_psi(0, True)
    spread_omega(0)
    send_psi(1, True)
    spread_omega(1)
    share_omega(0)
    for c in loads:
        c.wait()
    psi_arrived(0)
    left_products(0)
    omega_arrived(0)
    right_products(0)
    send_right(0)
    send_left(0)
    share_omega(1)
    psi_arrived(1)
    left_products(1)
    omega_arrived(1)
    right_products(1)
    send_right(1)
    send_left(1)
    pass_right(0)
    pass_right(1)
    sum_left(0)
    end_right(0)
    sum_left(1)
    end_right(1)

    for cond, c in pending:
        if cond is None:
            c.wait_send()
        else:
            @pl.when(cond)
            def _(c=c):
                c.wait_send()


def local(omega, psi, near_tiles, left_factors, right_factors, admissible, ranks):
    dma = pltpu.SemaphoreType.DMA
    anywhere = pl.BlockSpec(memory_space=pl.ANY)
    vmem = pl.BlockSpec(memory_space=pltpu.VMEM)
    out = jax.ShapeDtypeStruct((64, K), F32)
    return pl.pallas_call(
        kernel,
        out_shape=(out, out),
        in_specs=[anywhere] * 7,
        out_specs=(vmem, vmem),
        scratch_shapes=[
            pltpu.VMEM((2, 2, 1024, KH), BF16),
            pltpu.VMEM((2, 1024, KH), BF16),
            pltpu.VMEM((2, 256, KH), BF16),
            pltpu.VMEM((1024, 3 * TILE), BF16),
            pltpu.VMEM((1024, 256), BF16),
            pltpu.VMEM((128, 2048), BF16),
            pltpu.VMEM((2, 256, KH), BF16),
            pltpu.VMEM((4, 128, KH), BF16),
            pltpu.VMEM((2, 8, 2, 64, KH), F32),
            pltpu.VMEM((2, 8, 2, 64, KH), BF16),
            pltpu.VMEM((2, 8, 2, 64, KH), BF16),
            pltpu.VMEM((2, 64, KH), F32),
            pltpu.VMEM((2, 64, KH), F32),
            pltpu.VMEM((2, 16, 2, 64, KH), F32),
            pltpu.VMEM((2, 16, 64, KH), F32),
            pltpu.VMEM((2, 16, 64, KH), BF16),
            pltpu.VMEM((2, 16, 64, KH), BF16),
            pltpu.SMEM((2, 4), jnp.int32),
            pltpu.SMEM((2, 4), jnp.int32),
            dma((9,)), dma((2,)), dma((2,)), dma((2, 8)), dma((2, 4)), dma((2, 9)), dma((2, 4)), dma((2, 4)), dma((2, 4)),
            dma((2, 2, 8)), dma((2, 2, 8)), dma((2,)), dma((2,)), dma((2, 4)), dma((2, 4)),
            dma((2, 16)), dma((2, 16)),
        ],
        compiler_params=pltpu.CompilerParams(collective_id=0, has_side_effects=True,
                                             vmem_limit_bytes=64 << 20),
        cost_estimate=pl.CostEstimate(flops=2 * 10 ** 9, bytes_accessed=6 << 20, transcendentals=0),
    )(omega, psi, near_tiles, left_factors, right_factors, admissible, ranks)


def solution(mesh):
    return jax.shard_map(
        local,
        mesh=mesh,
        in_specs=(
            P("row", None),
            P("col", None),
            P("row", None),
            P("row", "col"),
            P("row", "col"),
            P("row", "col"),
            P("row", "col"),
        ),
        out_specs=(P(("row", "col"), None), P(("col", "row"), None)),
        check_vma=False,
    )
```

time: 663 us -> 59.2 us (0.09)
  the two profiles are of different devices: /device:TPU:16 before, /device:TPU:18 now
where the time goes in v3:
time: 59.2 us; the launch traced here: 59 us
  Pallas kernels  55.4 us (94%)
  local copies, waits for them, and re-layouts  2.95 us (5%)
  between operations  0.64 us (1%)
    pallas_call x1, Pallas kernels, local(): pl.pallas_call(kernel, out_shape=(out, out), in_specs=[anywhere] * 7, out...  55.4 us
    unnamed x2, local copies, waits for them, and re-layouts  2.95 us

profile of v3, /device:TPU:18, one launch (start us, length us, event | category | flops | bytes accessed | tf_op | source)
XLA Modules:
  0.0 59.0 jit_solution(12985136920622821833)
XLA Ops:
  0.6 55.4 %shard_map.86 = (f32[64,256]{1,0:T(8,128)}, f32[64,256]{1,0:T(8,128)}) custom-call(bf16[1024,256]{1,0:T(8,128)(2,1)} %omega.1, bf16[2048,256]{1,0:T(8,128)(2,1)} %psi.1, bf16[1024,1536]{1,0:T(8,128)(2,1)} %near.1, bf16[1024,256]{1,0:T(8,128)(2,1)} %left.1, bf16[128,2048]{1,0:T(8,128)(2,1)} %right.1, s32[2,4]{1,0:T(2,128)} %adm_in.1, s32[2,4]{1,0:T(2,128)} %ranks_in.1), custom_call_target="tpu_custom_call" | custom-call | flops 2000000000 | bytes 6291456 | tf_op jit(solution)/shard_map/pallas_call | solution.py:348
  56.1 1.5 %copy.11 = f32[64,256]{1,0:T(8,128)} copy(f32[64,256]{1,0:T(8,128)} %get-tuple-element.4) | data formatting | bytes 131072
  57.5 1.5 %copy.12 = f32[64,256]{1,0:T(8,128)} copy(f32[64,256]{1,0:T(8,128)} %get-tuple-element.5) | data formatting | bytes 131072

commit v4 on v3

--- a/solution.py
+++ b/solution.py
@@ -22,9 +22,9 @@
     return jnp.where(z == 4, 3, jnp.where(z == 3, 4, jnp.where(z == 6, 0, 7)))
 
 
-def kernel(omega, psi, near, left, right, adm_in, ranks_in, y_out, z_out,
-           om, ps, pr, nr, uu, vv, cr, cl, yp, y16, yr, yacc, yh, zp, zc, z16, zr,
-           adm, ranks, load_sem, pr_send, pr_recv, ps_send, ps_recv, om_send, om_recv, tw_send, tw_recv,
+def kernel(omega, psi, near, left, right, adm_in, ranks_in, r_out,
+           om, ps, pr, rb, nr, uu, vv, cr, cl, yp, y16, yr, yacc, yh, zp, zc, z16, zr,
+           adm, ranks, load_sem, pr_send, pr_recv, rb_send, rb_recv, ps_send, ps_recv, om_send, om_recv, tw_send, tw_recv,
            y_send, y_recv, h_send, h_recv, c_send, c_recv, z_send, z_recv):
     row = lax.axis_index("row")
     col = lax.axis_index("col")
@@ -36,13 +36,16 @@
     xs, qs = y // 2, (y % 2) * 2 + zh
     ps_y = 2 * x + zl // 2
     tx = y // 2
+    dist = (y - ps_y + 8) % 8
     serves = (y % 2) == (zl // 2)
     holds = zh == zl % 2
-    own_psi = serves & (x == tx)
+    own_psi = serves & (dist != 4)
     relayed = serves & jnp.logical_not(holds)
     rz = relay_source(z)
     tz = jnp.where(z == 3, 4, jnp.where(z == 4, 3, jnp.where(z == 0, 6, 1)))
     relays = jnp.where((z == 3) | (z == 7), y % 2 == 0, ((z == 4) | (z == 0)) & (y % 2 == 1))
+    steps = (2, 6)
+    passed = [((y + 8 - g) % 8) // 2 for g in steps]
     om_root = (x == xs) & (zl == qs)
     first = k == 0
 
@@ -63,15 +66,33 @@
         pl.semaphore_signal(barrier, inc=1, device_id=dev, device_id_type=MESH)
 
     count = 0
+    near_by = (dist <= 1) | (dist == 7)
     for i in range(4):
-        @pl.when(jnp.logical_not(own_psi & (x == i)))
+        remote_part = jnp.logical_not(own_psi & (x == i))
+
+        @pl.when(remote_part & near_by)
         def _(i=i):
             greet(device(i, zl, k, ps_y, zh))
 
+        @pl.when(remote_part & (dist >= 2) & (dist <= 4))
+        def _(i=i):
+            greet(device(i, zl, k, (ps_y + 2) % 8, zh))
+
+        @pl.when(remote_part & (dist >= 4) & (dist <= 6))
+        def _(i=i):
+            greet(device(i, zl, k, (ps_y + 6) % 8, zh))
+
+    @pl.when(serves)
+    def _():
+        for g in steps:
+            greet(device(x, zl, k, (y + g) % 8, zh))
+
     @pl.when(relayed)
     def _():
         greet(device(x, rz % 4, k, y, rz // 4))
-    count += jnp.where(relays, 1, 0) + jnp.where(serves, jnp.where(x == tx, 7, 8), 0)
+    count += jnp.where(relays, 1, 0) + jnp.where(serves, 11, 0)
+    for target in [tx] + passed:
+        count -= jnp.where(serves & (x == target), 1, 0)
 
     @pl.when(on_axis & (u != us))
     def _():
@@ -130,6 +151,16 @@
             def _():
                 c.start()
 
+    def flush():
+        for cond, c in pending:
+            if cond is None:
+                c.wait_send()
+            else:
+                @pl.when(cond)
+                def _(c=c):
+                    c.wait_send()
+        pending.clear()
+
     def arrived(buf, sem):
         remote(buf, buf, c_send.at[0, 0], sem, sibling).wait_recv()
 
@@ -142,6 +173,13 @@
 
     def own_psi_copy(h, src):
         return pltpu.make_async_copy(src, ps.at[h, my_quarter], load_sem.at[7 + h])
+
+    def psi_final(h, cond, src, target, there, sem, rows=None):
+        dst = my_quarter
+        if rows is not None:
+            src = src.at[pl.ds(rows, 128)]
+            dst = pl.ds(pl.multiple_of(x * 256 + rows, 128), 128)
+        start(cond, remote(src, ps.at[h, dst], ps_send.at[h, sem], ps_recv.at[h, x], device(target, zl, k, there, zh)))
 
     def send_psi(h, relay):
         cond = serves & (relayed if relay else holds)
@@ -150,13 +188,31 @@
             @pl.when(cond)
             def _():
                 arrived(pr.at[h], pr_recv.at[h])
-        for i in range(8):
-            start(cond & jnp.logical_not((x == tx) & (y == i)),
-                  remote(src, ps.at[h, my_quarter], ps_send.at[h, i], ps_recv.at[h, x], device(tx, zl, k, i, zh)))
+        for n, g in enumerate(steps):
+            start(cond, remote(src, rb.at[h, n], rb_send.at[h, n], rb_recv.at[h, n],
+                               device(x, zl, k, (y + g) % 8, zh)))
+        psi_final(h, cond, src, tx, (y + 1) % 8, 0)
+        psi_final(h, cond, src, tx, (y + 7) % 8, 1)
+        psi_final(h, cond & (x != tx), src, tx, y, 2)
 
         @pl.when(cond & (x == tx))
         def _():
             own_psi_copy(h, src).start()
+
+    def pass_psi(h, relay):
+        cond = serves & (relayed if relay else holds)
+        for n, g in enumerate(steps):
+            @pl.when(cond)
+            def _(n=n):
+                arrived(rb.at[h, n], rb_recv.at[h, n])
+            src, to, way = rb.at[h, n], passed[n], (1, 7)[n]
+            psi_final(h, cond, src, to, (y + way) % 8, 3 + 3 * n)
+            psi_final(h, cond, src, to, (y + 2 * way) % 8, 4 + 3 * n, 128 * n)
+            psi_final(h, cond & (x != to), src, to, y, 5 + 3 * n)
+
+            @pl.when(cond & (x == to))
+            def _(src=src):
+                own_psi_copy(h, src).start()
 
     def psi_arrived(h):
         for i in range(4):
@@ -249,12 +305,13 @@
                                device(p // 4, p % 4, k, y, zh)))
 
     def sum_left(h):
-        total = zc[h, place]
         for i in range(1, 16):
             p = (place + i) % 16
             arrived(zr.at[h, p], z_recv.at[h, p])
-            total += zr[h, p].astype(F32)
-        z_out[:, h * KH:(h + 1) * KH] = total
+            more = zr[h, p].astype(F32)
+            total = more if i == 1 else total + more
+        r_out[2, :, h * KH:(h + 1) * KH] = total
+        r_out[3, :, h * KH:(h + 1) * KH] = zc[h, place]
 
     def right_products(h):
         for b in range(4):
@@ -296,7 +353,8 @@
     def end_right(h):
         total = sum_right(h, zh)
         arrived(yh.at[h], h_recv.at[h])
-        y_out[:, h * KH:(h + 1) * KH] = total + yh[h]
+        r_out[0, :, h * KH:(h + 1) * KH] = total
+        r_out[1, :, h * KH:(h + 1) * KH] = yh[h]
 
     relay_psi(0)
     relay_psi(1)
@@ -305,9 +363,13 @@
     scatter_omega(1)
     send_psi(1, False)
     send_psi(0, True)
+    send_psi(1, True)
+    pass_psi(0, False)
+    pass_psi(1, False)
     spread_omega(0)
-    send_psi(1, True)
+    pass_psi(0, True)
     spread_omega(1)
+    pass_psi(1, True)
     share_omega(0)
     for c in loads:
         c.wait()
@@ -323,37 +385,41 @@
     omega_arrived(1)
     right_products(1)
     send_right(1)
+    rest = pending[:]
     send_left(1)
+    late = pending[len(rest):]
+    pending[:] = rest
+    flush()
+    pending[:] = late
     pass_right(0)
     pass_right(1)
+    last = pending[-2:]
+    del pending[-2:]
     sum_left(0)
+    flush()
+    pending[:] = last
+    sum_left(1)
     end_right(0)
-    sum_left(1)
     end_right(1)
 
-    for cond, c in pending:
-        if cond is None:
-            c.wait_send()
-        else:
-            @pl.when(cond)
-            def _(c=c):
-                c.wait_send()
+    flush()
 
 
 def local(omega, psi, near_tiles, left_factors, right_factors, admissible, ranks):
     dma = pltpu.SemaphoreType.DMA
     anywhere = pl.BlockSpec(memory_space=pl.ANY)
     vmem = pl.BlockSpec(memory_space=pltpu.VMEM)
-    out = jax.ShapeDtypeStruct((64, K), F32)
-    return pl.pallas_call(
+    out = jax.ShapeDtypeStruct((4, 64, K), F32)
+    parts = pl.pallas_call(
         kernel,
-        out_shape=(out, out),
+        out_shape=out,
         in_specs=[anywhere] * 7,
-        out_specs=(vmem, vmem),
+        out_specs=vmem,
         scratch_shapes=[
             pltpu.VMEM((2, 2, 1024, KH), BF16),
             pltpu.VMEM((2, 1024, KH), BF16),
             pltpu.VMEM((2, 256, KH), BF16),
+            pltpu.VMEM((2, 2, 256, KH), BF16),
             pltpu.VMEM((1024, 3 * TILE), BF16),
             pltpu.VMEM((1024, 256), BF16),
             pltpu.VMEM((128, 2048), BF16),
@@ -370,7 +436,7 @@
             pltpu.VMEM((2, 16, 64, KH), BF16),
             pltpu.SMEM((2, 4), jnp.int32),
             pltpu.SMEM((2, 4), jnp.int32),
-            dma((9,)), dma((2,)), dma((2,)), dma((2, 8)), dma((2, 4)), dma((2, 9)), dma((2, 4)), dma((2, 4)), dma((2, 4)),
+            dma((9,)), dma((2,)), dma((2,)), dma((2, 2)), dma((2, 2)), dma((2, 9)), dma((2, 4)), dma((2, 9)), dma((2, 4)), dma((2, 4)), dma((2, 4)),
             dma((2, 2, 8)), dma((2, 2, 8)), dma((2,)), dma((2,)), dma((2, 4)), dma((2, 4)),
             dma((2, 16)), dma((2, 16)),
         ],
@@ -378,6 +444,7 @@
                                              vmem_limit_bytes=64 << 20),
         cost_estimate=pl.CostEstimate(flops=2 * 10 ** 9, bytes_accessed=6 << 20, transcendentals=0),
     )(omega, psi, near_tiles, left_factors, right_factors, admissible, ranks)
+    return (parts[0] + parts[1], parts[2] + parts[3])
 
 
 def solution(mesh):

time: 59.2 us -> 57.3 us (0.968)
  the two profiles are of different devices: /device:TPU:18 before, /device:TPU:54 now
where the time goes in v4:
time: 57.3 us; the launch traced here: 57.1 us
  Pallas kernels  54.9 us (96%)
  other arithmetic  1.6 us (3%)
  between operations  0.64 us (1%)
    pallas_call x1, Pallas kernels, local(): pl.pallas_call(kernel, out_shape=out, in_specs=[anywhere] * 7, out_specs=...  54.9 us
    add x1, other arithmetic, local(): return (parts[0] + parts[1], parts[2] + parts[3])  1.6 us

profile of v4, /device:TPU:54, one launch (start us, length us, event | category | flops | bytes accessed | tf_op | source)
XLA Modules:
  0.0 57.1 jit_solution(17357788836731018977)
XLA Ops:
  0.6 54.9 %shard_map.86 = f32[4,64,256]{2,1,0:T(8,128)} custom-call(bf16[1024,256]{1,0:T(8,128)(2,1)} %omega.1, bf16[2048,256]{1,0:T(8,128)(2,1)} %psi.1, bf16[1024,1536]{1,0:T(8,128)(2,1)} %near.1, bf16[1024,256]{1,0:T(8,128)(2,1)} %left.1, bf16[128,2048]{1,0:T(8,128)(2,1)} %right.1, s32[2,4]{1,0:T(2,128)} %adm_in.1, s32[2,4]{1,0:T(2,128)} %ranks_in.1), custom_call_target="tpu_custom_call" | custom-call | flops 2000000000 | bytes 6291456 | tf_op jit(solution)/shard_map/pallas_call | solution.py:413
  55.5 1.6 %add_bitcast_fusion = (f32[64,256]{1,0:T(8,128)}, f32[64,256]{1,0:T(8,128)}) fusion(f32[4,64,256]{2,1,0:T(8,128)} %shard_map.86), kind=kLoop, calls=%fused_computation | loop fusion | flops 32768 | bytes 393216 | tf_op jit(solution)/shard_map/add | solution.py:447

commit v5 on v4

--- a/solution.py
+++ b/solution.py
@@ -23,7 +23,7 @@
 
 
 def kernel(omega, psi, near, left, right, adm_in, ranks_in, r_out,
-           om, ps, pr, rb, nr, uu, vv, cr, cl, yp, y16, yr, yacc, yh, zp, zc, z16, zr,
+           om, ps, pq, pr, rb, nr, uu, vv, cr, cl, yp, y16, yr, yacc, yh, zp, zc, z16, zr,
            adm, ranks, load_sem, pr_send, pr_recv, rb_send, rb_recv, ps_send, ps_recv, om_send, om_recv, tw_send, tw_recv,
            y_send, y_recv, h_send, h_recv, c_send, c_recv, z_send, z_recv):
     row = lax.axis_index("row")
@@ -131,6 +131,15 @@
             c.start()
     for c in loads:
         c.start()
+    root_psi = [pltpu.make_async_copy(psi.at[pl.ds(pl.multiple_of(k * 1024, 1024), 1024), pl.ds(h * KH, KH)], pq.at[h],
+                                      load_sem.at[9 + h]) for h in range(2)]
+
+    @pl.when(om_root)
+    def _():
+        for c in root_psi:
+            c.start()
+    yp[...] = jnp.zeros_like(yp)
+    zp[...] = jnp.zeros_like(zp)
     pl.semaphore_wait(barrier, count)
 
     @pl.when(om_root)
@@ -235,28 +244,36 @@
             j = (us + i) % 4
             send_omega(h, om_root, j, i - 1, at(j, vs))
 
-    def spread_omega(h):
+    def spread_omega(h, along):
+        cond = on_axis if along else jnp.logical_not(on_axis)
+
+        @pl.when(cond & jnp.logical_not(om_root))
+        def _():
+            arrived(quarter(h, u), om_recv.at[h, u])
+        if along:
+            for i in range(1, 4):
+                send_omega(h, on_axis, u, 2 + i, at(u, (v + i) % 4))
+        for i in range(1, 4):
+            j = (u + i) % 4
+            send_omega(h, cond & (j != us) if along else cond, u, 5 + i, at(j, v))
+        start(cond & jnp.logical_not(om_root),
+              remote(quarter(h, u), quarter(h, u), tw_send.at[h, 0], tw_recv.at[h, u], sibling))
+
+    def share_omega(h):
+        for i in range(1, 4):
+            j = (u + i) % 4
+
+            @pl.when(jnp.logical_not(om_root))
+            def _(j=j):
+                arrived(quarter(h, j), om_recv.at[h, j])
+            start(jnp.logical_not(om_root),
+                  remote(quarter(h, j), quarter(h, j), tw_send.at[h, i], tw_recv.at[h, j], sibling))
+
+    def omega_arrived(h):
         @pl.when(jnp.logical_not(om_root))
         def _():
-            arrived(quarter(h, u), om_recv.at[h, u])
-        for i in range(1, 4):
-            send_omega(h, on_axis, u, 2 + i, at(u, (v + i) % 4))
-        for i in range(1, 4):
-            j = (u + i) % 4
-            send_omega(h, jnp.logical_not(on_axis & (j == us)), u, 5 + i, at(j, v))
-
-    def share_omega(h):
-        for i in range(4):
-            j = (u + i) % 4
-            if i:
-                @pl.when(jnp.logical_not(om_root))
-                def _(j=j):
-                    arrived(quarter(h, j), om_recv.at[h, j])
-            start(None, remote(quarter(h, j), quarter(h, j), tw_send.at[h, j], tw_recv.at[h, j], sibling))
-
-    def omega_arrived(h):
-        for j in range(4):
-            arrived(om.at[1 - k, h, pl.ds(256 * j, 256)], tw_recv.at[h, j])
+            for j in range(4):
+                arrived(om.at[1 - k, h, pl.ds(256 * j, 256)], tw_recv.at[h, j])
 
     level = lax.broadcasted_iota(jnp.int32, (RMAX, KH), 0)
 
@@ -266,12 +283,40 @@
     def flag(a, b):
         return jnp.where(adm[a, b] == 0, 1.0, 0.0).astype(F32)
 
-    def dense(a, b, add):
-        off = 4 * col + b - (2 * row + a) + 1
-
-        @pl.when((off >= 0) & (off <= 2))
+    corners = {(0, 3): row == 2 * col + 2, (1, 0): row == 2 * col - 1}
+
+    def tile(a, off):
+        return nr[a * TILE:(a + 1) * TILE, pl.ds(pl.multiple_of(off * TILE, TILE), TILE)]
+
+    def add_right(h, a, b, block):
+        more = jnp.dot(block, om[b // 2, h, (b % 2) * TILE:(b % 2 + 1) * TILE, :], preferred_element_type=F32)
+        yp[h, 4 * a:4 * a + 4] += (more * flag(a, b)).reshape(4, 2, 64, KH)
+
+    def add_left(h, a, b, block, rows):
+        more = lax.dot_general(block, rows[h, a * TILE:(a + 1) * TILE, :], (((0,), (0,)), ((), ())),
+                               preferred_element_type=F32)
+        zp[h, 4 * b:4 * b + 4] += (more * flag(a, b)).reshape(4, 2, 64, KH)
+
+    def share_root():
+        for h in range(2):
+            start(om_root, remote(om.at[k, h], om.at[k, h], tw_send.at[h, 0], tw_recv.at[h, 0], sibling))
+
+    def diagonal_products():
+        @pl.when(om_root)
         def _():
-            add(nr[a * TILE:(a + 1) * TILE, pl.ds(pl.multiple_of(off * TILE, TILE), TILE)])
+            for c in root_psi:
+                c.wait()
+            for h in range(2):
+                arrived(om.at[1 - k, h], tw_recv.at[h, 0])
+            for a in range(2):
+                for b in range(4):
+                    off = b - 2 * k - a + 1
+
+                    @pl.when((off >= 0) & (off <= 2))
+                    def _(a=a, b=b, off=off):
+                        for h in range(2):
+                            add_right(h, a, b, tile(a, off))
+                            add_left(h, a, b, tile(a, off), pq)
 
     def left_products(h):
         for a in range(2):
@@ -283,13 +328,12 @@
         for b in range(4):
             part = lax.dot_general(vv[:, b * TILE:(b + 1) * TILE], cl[b], (((0,), (0,)), ((), ())),
                                    preferred_element_type=F32)
-            zp[h, 4 * b:4 * b + 4] = part.reshape(4, 2, 64, KH)
-            for a in range(2):
-                def add(block, a=a, b=b):
-                    more = lax.dot_general(block, ps[h, a * TILE:(a + 1) * TILE, :], (((0,), (0,)), ((), ())),
-                                           preferred_element_type=F32)
-                    zp[h, 4 * b:4 * b + 4] += (more * flag(a, b)).reshape(4, 2, 64, KH)
-                dense(a, b, add)
+            zp[h, 4 * b:4 * b + 4] += part.reshape(4, 2, 64, KH)
+            for a, corner, off in ((0, 3, 0), (1, 0, 2)):
+                if b == corner:
+                    @pl.when(corners[a, b])
+                    def _(a=a, b=b, off=off):
+                        add_left(h, a, b, tile(a, off), ps)
             start(None, remote(zp.at[h, pl.ds(4 * b, 4), 1 - k], zc.at[h, pl.ds(4 * b, 4)], c_send.at[h, b],
                                c_recv.at[h, b], sibling))
 
@@ -321,14 +365,13 @@
                 piece = full[a * RMAX:(a + 1) * RMAX]
                 cr[a, b * RMAX:(b + 1) * RMAX, :] = jnp.where(level < limit(a, b), piece, 0.0).astype(BF16)
         for a in range(2):
-            yp[h, 4 * a:4 * a + 4] = jnp.dot(uu[a * TILE:(a + 1) * TILE, :], cr[a],
-                                             preferred_element_type=F32).reshape(4, 2, 64, KH)
-            for b in range(4):
-                def add(block, a=a, b=b):
-                    more = jnp.dot(block, om[b // 2, h, (b % 2) * TILE:(b % 2 + 1) * TILE, :],
-                                   preferred_element_type=F32)
-                    yp[h, 4 * a:4 * a + 4] += (more * flag(a, b)).reshape(4, 2, 64, KH)
-                dense(a, b, add)
+            yp[h, 4 * a:4 * a + 4] += jnp.dot(uu[a * TILE:(a + 1) * TILE, :], cr[a],
+                                              preferred_element_type=F32).reshape(4, 2, 64, KH)
+            b, off = ((3, 0), (0, 2))[a]
+
+            @pl.when(corners[a, b])
+            def _(a=a, b=b, off=off):
+                add_right(h, a, b, tile(a, off))
             y16[h, 4 * a:4 * a + 4] = yp[h, 4 * a:4 * a + 4].astype(BF16)
 
     def send_right(h):
@@ -356,35 +399,39 @@
         r_out[0, :, h * KH:(h + 1) * KH] = total
         r_out[1, :, h * KH:(h + 1) * KH] = yh[h]
 
+    scatter_omega(0)
+    scatter_omega(1)
     relay_psi(0)
     relay_psi(1)
-    scatter_omega(0)
-    send_psi(0, False)
-    scatter_omega(1)
-    send_psi(1, False)
-    send_psi(0, True)
-    send_psi(1, True)
-    pass_psi(0, False)
-    pass_psi(1, False)
-    spread_omega(0)
-    pass_psi(0, True)
-    spread_omega(1)
-    pass_psi(1, True)
-    share_omega(0)
+    send_psi(0,False)
+    spread_omega(0,True)
+    spread_omega(1,True)
+    share_root()
+    send_psi(0,True)
+    pass_psi(0,False)
+    spread_omega(0,False)
+    send_psi(1,False)
+    pass_psi(0,True)
+    spread_omega(1,False)
+    send_psi(1,True)
+    pass_psi(1,False)
+    pass_psi(1,True)
     for c in loads:
         c.wait()
-    psi_arrived(0)
-    left_products(0)
+    diagonal_products()
+    share_omega(0)
     omega_arrived(0)
     right_products(0)
     send_right(0)
+    psi_arrived(0)
+    left_products(0)
+    share_omega(1)
     send_left(0)
-    share_omega(1)
-    psi_arrived(1)
-    left_products(1)
     omega_arrived(1)
     right_products(1)
     send_right(1)
+    psi_arrived(1)
+    left_products(1)
     rest = pending[:]
     send_left(1)
     late = pending[len(rest):]
@@ -417,6 +464,7 @@
         out_specs=vmem,
         scratch_shapes=[
             pltpu.VMEM((2, 2, 1024, KH), BF16),
+            pltpu.VMEM((2, 1024, KH), BF16),
             pltpu.VMEM((2, 1024, KH), BF16),
             pltpu.VMEM((2, 256, KH), BF16),
             pltpu.VMEM((2, 2, 256, KH), BF16),
@@ -436,7 +484,7 @@
             pltpu.VMEM((2, 16, 64, KH), BF16),
             pltpu.SMEM((2, 4), jnp.int32),
             pltpu.SMEM((2, 4), jnp.int32),
-            dma((9,)), dma((2,)), dma((2,)), dma((2, 2)), dma((2, 2)), dma((2, 9)), dma((2, 4)), dma((2, 9)), dma((2, 4)), dma((2, 4)), dma((2, 4)),
+            dma((11,)), dma((2,)), dma((2,)), dma((2, 2)), dma((2, 2)), dma((2, 9)), dma((2, 4)), dma((2, 9)), dma((2, 4)), dma((2, 4)), dma((2, 4)),
             dma((2, 2, 8)), dma((2, 2, 8)), dma((2,)), dma((2,)), dma((2, 4)), dma((2, 4)),
             dma((2, 16)), dma((2, 16)),
         ],

time: 57.3 us -> 56.3 us (0.983)
  the two profiles are of different devices: /device:TPU:54 before, /device:TPU:136 now
where the time goes in v5:
time: 56.3 us; the launch traced here: 56.1 us
  Pallas kernels  53.9 us (96%)
  other arithmetic  1.6 us (3%)
  between operations  0.64 us (1%)
    pallas_call x1, Pallas kernels, local(): pl.pallas_call(kernel, out_shape=out, in_specs=[anywhere] * 7, out_specs=...  53.9 us
    add x1, other arithmetic, local(): return (parts[0] + parts[1], parts[2] + parts[3])  1.6 us

profile of v5, /device:TPU:136, one launch (start us, length us, event | category | flops | bytes accessed | tf_op | source)
XLA Modules:
  0.0 56.1 jit_solution(7739762745264441147)
XLA Ops:
  0.6 53.9 %shard_map.86 = f32[4,64,256]{2,1,0:T(8,128)} custom-call(bf16[1024,256]{1,0:T(8,128)(2,1)} %omega.1, bf16[2048,256]{1,0:T(8,128)(2,1)} %psi.1, bf16[1024,1536]{1,0:T(8,128)(2,1)} %near.1, bf16[1024,256]{1,0:T(8,128)(2,1)} %left.1, bf16[128,2048]{1,0:T(8,128)(2,1)} %right.1, s32[2,4]{1,0:T(2,128)} %adm_in.1, s32[2,4]{1,0:T(2,128)} %ranks_in.1), custom_call_target="tpu_custom_call" | custom-call | flops 2000000000 | bytes 6291456 | tf_op jit(solution)/shard_map/pallas_call | solution.py:460
  54.5 1.6 %add_bitcast_fusion = (f32[64,256]{1,0:T(8,128)}, f32[64,256]{1,0:T(8,128)}) fusion(f32[4,64,256]{2,1,0:T(8,128)} %shard_map.86), kind=kLoop, calls=%fused_computation | loop fusion | flops 32768 | bytes 393216 | tf_op jit(solution)/shard_map/add | solution.py:495
